TPU v7x, 32 devices: a whole 2x2x4 slice. The times are simulated.
32 devices in a mesh: slab: 16 (over z, y, x), col: 2 (over core).
Axes of the slice: x: 2, y: 2, z: 4, core: 2. Of those that a mesh axis runs over, the one named last changes fastest.
Arguments:
- coupling: float32 [16, 512, 512], P('slab', None, 'col'), as said below
- tile_pattern: int32 [16, 4, 4], P('slab', None, 'col'), may hold values from 0 to 1, as said below
- orbital_mass: float32 [16, 512], P('slab', 'col'), may hold values from 0.0001 to 0.05
- sources: float32 [16, 512, 256], P('slab', None, 'col'), may hold values from -0.3 to 0.3
Outputs:
- solution: float32 [16, 512, 256], P('slab', None, 'col')
Inputs may be any that keep to these rules, and one draw needn't show every extreme that they name: Each coupling block is symmetric and positive semidefinite. `tile_pattern`: in each slab every tile belongs to one group, and two tiles are linked exactly when they share a group, so each pattern is symmetric with ones on its diagonal.
All inputs are finite; a program needn't handle non-finite values.
Results may differ from a plain program's by a relative error of at most 0.0003.
Values sent between devices are 32-bit elements; how exact they have to be, the bound alone decides.
No kernel may reach another device: no remote copies, remote signals or barrier semaphores. Data moves between devices by JAX's collectives and lax.ppermute only.
A program may use at most 128 MiB of HBM per device.

v0:
```python
import jax
import jax.numpy as jnp
from jax import lax
from jax.sharding import PartitionSpec as P

LEVELS = 6


leaf_limit = 128


def from_behind(shard, axis, by):
    size = lax.axis_size(axis)
    pairs = [(i, i + by) for i in range(size) if 0 <= i + by < size]
    return lax.ppermute(shard, axis, pairs)


def factor_inverse(matrix):
    width = matrix.shape[-1]
    if width <= leaf_limit:
        factor = jnp.linalg.cholesky(matrix)
        unit = jnp.eye(width, dtype=matrix.dtype)
        return lax.linalg.triangular_solve(factor, unit, left_side=True, lower=True)
    half_w = width // 2
    top_left = matrix[:half_w, :half_w]
    bottom_left = matrix[half_w:, :half_w]
    bottom_right = matrix[half_w:, half_w:]
    first_inv = factor_inverse(top_left)
    lower_part = jnp.dot(
        bottom_left,
        first_inv.T,
        precision=lax.Precision.HIGHEST,
        preferred_element_type=jnp.float32,
    )
    schur_part = bottom_right - jnp.dot(
        lower_part,
        lower_part.T,
        precision=lax.Precision.HIGHEST,
        preferred_element_type=jnp.float32,
    )
    second_inv = factor_inverse(schur_part)
    cross = -jnp.dot(
        second_inv,
        jnp.dot(
            lower_part,
            first_inv,
            precision=lax.Precision.HIGHEST,
            preferred_element_type=jnp.float32,
        ),
        precision=lax.Precision.HIGHEST,
        preferred_element_type=jnp.float32,
    )
    upper_row = jnp.concatenate(
        [first_inv, jnp.zeros((half_w, width - half_w), jnp.float32)], axis=1
    )
    lower_row = jnp.concatenate([cross, second_inv], axis=1)
    return jnp.concatenate([upper_row, lower_row], axis=0)


def solve_spd(matrix, rhs):
    inverse = factor_inverse(matrix)
    inner = jnp.dot(
        inverse, rhs, precision=lax.Precision.HIGHEST, preferred_element_type=jnp.float32
    )
    return jnp.dot(
        inverse.T, inner, precision=lax.Precision.HIGHEST, preferred_element_type=jnp.float32
    )


def on_device(coupling, tile_pattern, orbital_mass, sources):
    width = coupling.shape[1]
    half = coupling.shape[2]
    tiles_row = tile_pattern.shape[1]
    tiles_col = tile_pattern.shape[2]
    tile_width = width // tiles_row
    column = lax.axis_index("col")
    slab_index = lax.axis_index("slab")
    slab_count = lax.axis_size("slab")
    tile_mask = jnp.broadcast_to(
        tile_pattern[0][:, None, :, None].astype(jnp.float32),
        (tiles_row, tile_width, tiles_col, tile_width),
    ).reshape(width, half)
    row_ids = lax.broadcasted_iota(jnp.int32, (width, half), 0)
    col_ids = lax.broadcasted_iota(jnp.int32, (width, half), 1) + column * half
    unit_panel = (row_ids == col_ids).astype(jnp.float32)
    bond_panel = unit_panel + tile_mask * coupling[0]
    prior_panel = from_behind(bond_panel, "slab", 1)
    keep_upper = (slab_index < slab_count - 1).astype(jnp.float32)
    lower_panel = -prior_panel
    upper_panel = -bond_panel * keep_upper
    diag_panel = bond_panel + prior_panel + unit_panel * orbital_mass[0][None, :]
    source_panel = sources[0]
    for level_num in range(LEVELS):
        stride = 2**level_num
        if stride >= slab_count:
            break
        full_diag, full_lower, full_upper = (
            lax.all_gather(diag_panel, "col", axis=1, tiled=True),
            lax.all_gather(lower_panel, "col", axis=1, tiled=True),
            lax.all_gather(upper_panel, "col", axis=1, tiled=True),
        )
        solved = solve_spd(
            full_diag, jnp.concatenate([upper_panel, lower_panel, source_panel], axis=1)
        )
        from_below = from_behind(solved, "slab", stride)
        from_above = from_behind(solved, "slab", -stride)
        below_prod = jnp.dot(
            full_lower,
            from_below,
            precision=lax.Precision.HIGHEST,
            preferred_element_type=jnp.float32,
        )
        above_prod = jnp.dot(
            full_upper,
            from_above,
            precision=lax.Precision.HIGHEST,
            preferred_element_type=jnp.float32,
        )
        diag_panel = diag_panel - below_prod[:, :half] - above_prod[:, half : 2 * half]
        lower_panel = -below_prod[:, half : 2 * half]
        upper_panel = -above_prod[:, :half]
        source_panel = source_panel - below_prod[:, 2 * half :] - above_prod[:, 2 * half :]
    final_diag = lax.all_gather(diag_panel, "col", axis=1, tiled=True)
    solution = solve_spd(final_diag, source_panel)
    return solution[None]


def solution(mesh):
    placed = (
        P("slab", None, "col"),
        P("slab", None, "col"),
        P("slab", "col"),
        P("slab", None, "col"),
    )
    return jax.shard_map(
        on_device, mesh=mesh, in_specs=placed, out_specs=P("slab", None, "col"), check_vma=False
    )
```

profile of v0, /device:TPU:16, one launch (start us, length us, event | category | flops | bytes accessed | tf_op | source)
XLA Modules:
  0.0 917.8 jit_solution(6809934369462343896)
XLA Ops:
  12.2 13.9 %collective-permute-done = f32[512,256]{0,1:T(8,128)S(1)} collective-permute-done((f32[512,256]{0,1:T(8,128)S(1)}, f32[512,256]{0,1:T(8,128)S(1)}, u32[]{:S(2)}, u32[]{:S(2)}) %collective-permute-start) | collective-permute-done | bytes 524320 | tf_op jit(solution)/shard_map/ppermute | solution.py:15
  37.9 11.7 %cholesky.314 = f32[128,128]{1,0:T(8,128)S(1)} custom-call(f32[128,128]{1,0:T(8,128)S(1)} %fusion.184), custom_call_target="Cholesky" | custom-call | tf_op jit(solution)/shard_map/jit(cholesky)/cholesky | solution.py:21
  63.6 11.7 %cholesky.325 = f32[128,128]{1,0:T(8,128)S(1)} custom-call(f32[128,128]{1,0:T(8,128)S(1)} %fusion.182), custom_call_target="Cholesky" | custom-call | tf_op jit(solution)/shard_map/jit(cholesky)/cholesky | solution.py:21
  76.7 10.0 %custom-call.25 = f32[1,128,128]{1,2,0:T(8,128)S(1)} custom-call(f32[1,128,128]{2,1,0:T(8,128)S(1)} %fusion.106), custom_call_target="InvertDiagBlocksLowerTriangular" | custom-call | tf_op jit(solution)/shard_map/triangular_solve/custom-call.0 | solution.py:23
  89.0 11.7 %cholesky.336 = f32[128,128]{1,0:T(8,128)S(1)} custom-call(f32[128,128]{1,0:T(8,128)S(1)} %fusion.180), custom_call_target="Cholesky" | custom-call | tf_op jit(solution)/shard_map/jit(cholesky)/cholesky | solution.py:21
  113.0 23.4 %cholesky.347 = f32[128,128]{1,0:T(8,128)S(1)} custom-call(f32[128,128]{1,0:T(8,128)S(1)} %fusion.178), custom_call_target="Cholesky" | custom-call | tf_op jit(solution)/shard_map/jit(cholesky)/cholesky | solution.py:21
  162.9 52.5 %collective-permute-done.1 = f32[512,640]{1,0:T(8,128)S(1)} collective-permute-done((f32[512,640]{1,0:T(8,128)}, f32[512,640]{1,0:T(8,128)S(1)}, u32[]{:S(2)}, u32[]{:S(2)}) %collective-permute-start.1) | collective-permute-done | bytes 1310752 | tf_op jit(solution)/shard_map/ppermute | solution.py:15
  242.4 11.7 %cholesky.358 = f32[128,128]{1,0:T(8,128)S(1)} custom-call(f32[128,128]{1,0:T(8,128)S(1)} %fusion.176), custom_call_target="Cholesky" | custom-call | tf_op jit(solution)/shard_map/jit(cholesky)/cholesky | solution.py:21
  268.1 11.7 %cholesky.369 = f32[128,128]{1,0:T(8,128)S(1)} custom-call(f32[128,128]{1,0:T(8,128)S(1)} %fusion.174), custom_call_target="Cholesky" | custom-call | tf_op jit(solution)/shard_map/jit(cholesky)/cholesky | solution.py:21
  281.2 10.0 %custom-call.29 = f32[1,128,128]{1,2,0:T(8,128)S(1)} custom-call(f32[1,128,128]{2,1,0:T(8,128)S(1)} %fusion.110), custom_call_target="InvertDiagBlocksLowerTriangular" | custom-call | tf_op jit(solution)/shard_map/triangular_solve/custom-call.0 | solution.py:23
  293.4 11.7 %cholesky.380 = f32[128,128]{1,0:T(8,128)S(1)} custom-call(f32[128,128]{1,0:T(8,128)S(1)} %fusion.172), custom_call_target="Cholesky" | custom-call | tf_op jit(solution)/shard_map/jit(cholesky)/cholesky | solution.py:21
  317.5 12.1 %cholesky.391 = f32[128,128]{1,0:T(8,128)S(1)} custom-call(f32[128,128]{1,0:T(8,128)S(1)} %fusion.170), custom_call_target="Cholesky" | custom-call | tf_op jit(solution)/shard_map/jit(cholesky)/cholesky | solution.py:21
  355.2 53.4 %collective-permute-done.3 = f32[512,640]{1,0:T(8,128)S(1)} collective-permute-done((f32[512,640]{1,0:T(8,128)}, f32[512,640]{1,0:T(8,128)S(1)}, u32[]{:S(2)}, u32[]{:S(2)}) %collective-permute-start.3) | collective-permute-done | bytes 1310752 | tf_op jit(solution)/shard_map/ppermute | solution.py:15
  436.3 11.7 %cholesky.402 = f32[128,128]{1,0:T(8,128)S(1)} custom-call(f32[128,128]{1,0:T(8,128)S(1)} %fusion.168), custom_call_target="Cholesky" | custom-call | tf_op jit(solution)/shard_map/jit(cholesky)/cholesky | solution.py:21
  461.9 11.7 %cholesky.413 = f32[128,128]{1,0:T(8,128)S(1)} custom-call(f32[128,128]{1,0:T(8,128)S(1)} %fusion.166), custom_call_target="Cholesky" | custom-call | tf_op jit(solution)/shard_map/jit(cholesky)/cholesky | solution.py:21
  474.9 10.2 %custom-call.33 = f32[1,128,128]{1,2,0:T(8,128)S(1)} custom-call(f32[1,128,128]{2,1,0:T(8,128)S(1)} %fusion.114), custom_call_target="InvertDiagBlocksLowerTriangular" | custom-call | tf_op jit(solution)/shard_map/triangular_solve/custom-call.0 | solution.py:23
  487.3 11.7 %cholesky.424 = f32[128,128]{1,0:T(8,128)S(1)} custom-call(f32[128,128]{1,0:T(8,128)S(1)} %fusion.164), custom_call_target="Cholesky" | custom-call | tf_op jit(solution)/shard_map/jit(cholesky)/cholesky | solution.py:21
  511.3 11.9 %cholesky.435 = f32[128,128]{1,0:T(8,128)S(1)} custom-call(f32[128,128]{1,0:T(8,128)S(1)} %fusion.162), custom_call_target="Cholesky" | custom-call | tf_op jit(solution)/shard_map/jit(cholesky)/cholesky | solution.py:21
  547.8 27.1 %collective-permute-done.5 = f32[512,640]{1,0:T(8,128)S(1)} collective-permute-done((f32[512,640]{1,0:T(8,128)}, f32[512,640]{1,0:T(8,128)S(1)}, u32[]{:S(2)}, u32[]{:S(2)}) %collective-permute-start.5) | collective-permute-done | bytes 1310752 | tf_op jit(solution)/shard_map/ppermute | solution.py:15
  602.6 11.7 %cholesky.446 = f32[128,128]{1,0:T(8,128)S(1)} custom-call(f32[128,128]{1,0:T(8,128)S(1)} %fusion.160), custom_call_target="Cholesky" | custom-call | tf_op jit(solution)/shard_map/jit(cholesky)/cholesky | solution.py:21
  628.5 11.7 %cholesky.457 = f32[128,128]{1,0:T(8,128)S(1)} custom-call(f32[128,128]{1,0:T(8,128)S(1)} %fusion.158), custom_call_target="Cholesky" | custom-call | tf_op jit(solution)/shard_map/jit(cholesky)/cholesky | solution.py:21
  641.7 10.0 %custom-call.37 = f32[1,128,128]{1,2,0:T(8,128)S(1)} custom-call(f32[1,128,128]{2,1,0:T(8,128)S(1)} %fusion.118), custom_call_target="InvertDiagBlocksLowerTriangular" | custom-call | tf_op jit(solution)/shard_map/triangular_solve/custom-call.0 | solution.py:23
  653.8 11.7 %cholesky.468 = f32[128,128]{1,0:T(8,128)S(1)} custom-call(f32[128,128]{1,0:T(8,128)S(1)} %fusion.156), custom_call_target="Cholesky" | custom-call | tf_op jit(solution)/shard_map/jit(cholesky)/cholesky | solution.py:21
  678.0 11.9 %cholesky.479 = f32[128,128]{1,0:T(8,128)S(1)} custom-call(f32[128,128]{1,0:T(8,128)S(1)} %fusion.154), custom_call_target="Cholesky" | custom-call | tf_op jit(solution)/shard_map/jit(cholesky)/cholesky | solution.py:21
  717.3 25.7 %collective-permute-done.7 = f32[512,640]{1,0:T(8,128)S(1)} collective-permute-done((f32[512,640]{1,0:T(8,128)}, f32[512,640]{1,0:T(8,128)S(1)}, u32[]{:S(2)}, u32[]{:S(2)}) %collective-permute-start.7) | collective-permute-done | bytes 1310752 | tf_op jit(solution)/shard_map/ppermute | solution.py:15
  746.5 25.8 %collective-permute-done.8 = f32[512,640]{1,0:T(8,128)} collective-permute-done((f32[512,640]{1,0:T(8,128)}, f32[512,640]{1,0:T(8,128)}, u32[]{:S(2)}, u32[]{:S(2)}) %collective-permute-start.8) | collective-permute-done | bytes 1310752 | tf_op jit(solution)/shard_map/ppermute | solution.py:15
  777.2 12.6 %all-gather.38.cloned.1.call-done = f32[512,512]{0,1:T(8,128)} async-done(((f32[512,256]{0,1:T(8,128)}), f32[512,512]{0,1:T(8,128)}) %all-gather.38.cloned.1.call-update) | async-done | bytes 1048592 | tf_op jit(solution)/shard_map/all_gather | solution.py:123
  791.6 11.7 %cholesky.490 = f32[128,128]{1,0:T(8,128)S(1)} custom-call(f32[128,128]{1,0:T(8,128)S(1)} %fusion.152), custom_call_target="Cholesky" | custom-call | tf_op jit(solution)/shard_map/jit(cholesky)/cholesky | solution.py:21
  817.3 11.9 %cholesky.501 = f32[128,128]{1,0:T(8,128)S(1)} custom-call(f32[128,128]{1,0:T(8,128)S(1)} %fusion.150), custom_call_target="Cholesky" | custom-call | tf_op jit(solution)/shard_map/jit(cholesky)/cholesky | solution.py:21
  848.0 13.2 %cholesky.512 = f32[128,128]{1,0:T(8,128)} custom-call(f32[128,128]{1,0:T(8,128)} %fusion.148), custom_call_target="Cholesky" | custom-call | tf_op jit(solution)/shard_map/jit(cholesky)/cholesky | solution.py:21
  864.8 11.5 %custom-call.42 = f32[1,128,128]{1,2,0:T(8,128)} custom-call(f32[1,128,128]{2,1,0:T(8,128)} %fusion.123), custom_call_target="InvertDiagBlocksLowerTriangular" | custom-call | tf_op jit(solution)/shard_map/triangular_solve/custom-call.0 | solution.py:23
  882.8 11.7 %cholesky.523 = f32[128,128]{1,0:T(8,128)S(1)} custom-call(f32[128,128]{1,0:T(8,128)S(1)} %fusion.146), custom_call_target="Cholesky" | custom-call | tf_op jit(solution)/shard_map/jit(cholesky)/cholesky | solution.py:21
  (382 shorter events, 391.2 us)
Async XLA Ops:
  6.5 29.5 %all-gather.16.cloned.1.call-start = ((), (), s32[]{:S(2)}) async-start(), calls=%async_computation.1 | async-start | bytes 1572864 | tf_op jit(solution)/shard_map/all_gather | solution.py:98
  8.8 139.9 %copy-start.12 = (f32[512,256]{0,1:T(8,128)}, f32[512,256]{0,1:T(8,128)S(1)}, u32[]{:S(2)}) copy-start(f32[512,256]{0,1:T(8,128)S(1)} %get-tuple-element.6) | copy-start | bytes 1572868
  8.8 17.4 %collective-permute-start = (f32[512,256]{0,1:T(8,128)S(1)}, f32[512,256]{0,1:T(8,128)S(1)}, u32[]{:S(2)}, u32[]{:S(2)}) collective-permute-start(f32[512,256]{0,1:T(8,128)S(1)} %get-tuple-element.8), channel_id=1, source_target_pairs={{0,2},{2,4},{4,6},{6,8},{8,10},{10,12},{12,14},{14,16},{16,18},{18... | collective-permute-start | bytes 1572872 | tf_op jit(solution)/shard_map/ppermute | solution.py:15
  27.3 135.6 %all-gather.14.cloned.1.call-start = ((), (), s32[]{:S(2)}) async-start(), calls=%async_computation | async-start | bytes 1572864 | tf_op jit(solution)/shard_map/all_gather | solution.py:99
  28.1 193.3 %all-gather.18.cloned.1.call-start = ((), (), s32[]{:S(2)}) async-start(), calls=%async_computation.2 | async-start | bytes 1572864 | tf_op jit(solution)/shard_map/all_gather | solution.py:100
  36.0 51.4 %copy-start.18 = (f32[512,512]{0,1:T(8,128)S(1)}, f32[512,512]{0,1:T(8,128)}, u32[]{:S(2)}) copy-start(f32[512,512]{0,1:T(8,128)} %all-gather.16.cloned.1.call-done) | copy-start | bytes 3145732
  112.6 36.1 %copy-start.6 = (f32[512,256]{0,1:T(8,128)S(1)}, f32[512,256]{0,1:T(8,128)}, u32[]{:S(2)}) copy-start(f32[512,256]{0,1:T(8,128)} %get-tuple-element.22) | copy-start | bytes 1572868
  155.2 60.3 %collective-permute-start.1 = (f32[512,640]{1,0:T(8,128)}, f32[512,640]{1,0:T(8,128)S(1)}, u32[]{:S(2)}, u32[]{:S(2)}) collective-permute-start(f32[512,640]{1,0:T(8,128)} %fusion.65), channel_id=1, source_target_pairs={{0,2},{2,4},{4,6},{6,8},{8,10},{10,12},{12,14},{14,16},{16,18},{18... | collective-permute-start | bytes 3932168 | tf_op jit(solution)/shard_map/ppermute | solution.py:15
  158.6 62.8 %collective-permute-start.2 = (f32[512,640]{1,0:T(8,128)}, f32[512,640]{1,0:T(8,128)}, u32[]{:S(2)}, u32[]{:S(2)}) collective-permute-start(f32[512,640]{1,0:T(8,128)} %fusion.65), channel_id=1, source_target_pairs={{2,0},{4,2},{6,4},{8,6},{10,8},{12,10},{14,12},{16,14},{18,16},{20... | collective-permute-start | bytes 3932168 | tf_op jit(solution)/shard_map/ppermute | solution.py:15
  162.9 77.7 %all-gather.22.cloned.1.call-start = ((), (), s32[]{:S(2)}) async-start(), calls=%async_computation.4 | async-start | bytes 1572864 | tf_op jit(solution)/shard_map/all_gather | solution.py:98
  231.1 124.1 %all-gather.20.cloned.1.call-start = ((), (), s32[]{:S(2)}) async-start(), calls=%async_computation.3 | async-start | bytes 1572864 | tf_op jit(solution)/shard_map/all_gather | solution.py:99
  231.7 182.7 %all-gather.24.cloned.1.call-start = ((), (), s32[]{:S(2)}) async-start(), calls=%async_computation.5 | async-start | bytes 1572864 | tf_op jit(solution)/shard_map/all_gather | solution.py:100
  240.5 51.3 %copy-start.15 = (f32[512,512]{0,1:T(8,128)S(1)}, f32[512,512]{0,1:T(8,128)}, u32[]{:S(2)}) copy-start(f32[512,512]{0,1:T(8,128)} %all-gather.22.cloned.1.call-done) | copy-start | bytes 3145732
  317.0 24.8 %copy-start.7 = (f32[512,256]{1,0:T(8,128)S(1)}, f32[512,256]{1,0:T(8,128)}, u32[]{:S(2)}) copy-start(f32[512,256]{1,0:T(8,128)} %get-tuple-element.18) | copy-start | bytes 1572868
  317.1 24.8 %copy-start.10 = (f32[512,256]{1,0:T(8,128)S(1)}, f32[512,256]{1,0:T(8,128)}, u32[]{:S(2)}) copy-start(f32[512,256]{1,0:T(8,128)} %get-tuple-element.20) | copy-start | bytes 1572868
  348.3 60.3 %collective-permute-start.3 = (f32[512,640]{1,0:T(8,128)}, f32[512,640]{1,0:T(8,128)S(1)}, u32[]{:S(2)}, u32[]{:S(2)}) collective-permute-start(f32[512,640]{1,0:T(8,128)} %fusion.66), channel_id=1, source_target_pairs={{0,4},{2,6},{4,8},{6,10},{8,12},{10,14},{12,16},{14,18},{16,20},{1... | collective-permute-start | bytes 3932168 | tf_op jit(solution)/shard_map/ppermute | solution.py:15
  351.7 62.7 %collective-permute-start.4 = (f32[512,640]{1,0:T(8,128)}, f32[512,640]{1,0:T(8,128)}, u32[]{:S(2)}, u32[]{:S(2)}) collective-permute-start(f32[512,640]{1,0:T(8,128)} %fusion.66), channel_id=1, source_target_pairs={{4,0},{6,2},{8,4},{10,6},{12,8},{14,10},{16,12},{18,14},{20,16},{2... | collective-permute-start | bytes 3932168 | tf_op jit(solution)/shard_map/ppermute | solution.py:15
  355.1 79.3 %all-gather.28.cloned.1.call-start = ((), (), s32[]{:S(2)}) async-start(), calls=%async_computation.7 | async-start | bytes 1572864 | tf_op jit(solution)/shard_map/all_gather | solution.py:98
  424.0 123.7 %all-gather.26.cloned.1.call-start = ((), (), s32[]{:S(2)}) async-start(), calls=%async_computation.6 | async-start | bytes 1572864 | tf_op jit(solution)/shard_map/all_gather | solution.py:99
  424.8 156.0 %all-gather.30.cloned.1.call-start = ((), (), s32[]{:S(2)}) async-start(), calls=%async_computation.8 | async-start | bytes 1572864 | tf_op jit(solution)/shard_map/all_gather | solution.py:100
  434.4 51.4 %copy-start.16 = (f32[512,512]{0,1:T(8,128)S(1)}, f32[512,512]{0,1:T(8,128)}, u32[]{:S(2)}) copy-start(f32[512,512]{0,1:T(8,128)} %all-gather.28.cloned.1.call-done) | copy-start | bytes 3145732
  541.9 33.1 %collective-permute-start.5 = (f32[512,640]{1,0:T(8,128)}, f32[512,640]{1,0:T(8,128)S(1)}, u32[]{:S(2)}, u32[]{:S(2)}) collective-permute-start(f32[512,640]{1,0:T(8,128)} %fusion.67), channel_id=1, source_target_pairs={{0,8},{2,10},{4,12},{6,14},{8,16},{10,18},{12,20},{14,22},{16,24},... | collective-permute-start | bytes 3932168 | tf_op jit(solution)/shard_map/ppermute | solution.py:15
  545.2 35.5 %collective-permute-start.6 = (f32[512,640]{1,0:T(8,128)}, f32[512,640]{1,0:T(8,128)}, u32[]{:S(2)}, u32[]{:S(2)}) collective-permute-start(f32[512,640]{1,0:T(8,128)} %fusion.67), channel_id=1, source_target_pairs={{8,0},{10,2},{12,4},{14,6},{16,8},{18,10},{20,12},{22,14},{24,16},... | collective-permute-start | bytes 3932168 | tf_op jit(solution)/shard_map/ppermute | solution.py:15
  547.7 53.0 %all-gather.34.cloned.1.call-start = ((), (), s32[]{:S(2)}) async-start(), calls=%async_computation.10 | async-start | bytes 1572864 | tf_op jit(solution)/shard_map/all_gather | solution.py:98
  590.4 126.9 %all-gather.32.cloned.1.call-start = ((), (), s32[]{:S(2)}) async-start(), calls=%async_computation.9 | async-start | bytes 1572864 | tf_op jit(solution)/shard_map/all_gather | solution.py:99
  592.2 154.2 %all-gather.36.cloned.1.call-start = ((), (), s32[]{:S(2)}) async-start(), calls=%async_computation.11 | async-start | bytes 1572864 | tf_op jit(solution)/shard_map/all_gather | solution.py:100
  600.7 51.5 %copy-start.17 = (f32[512,512]{0,1:T(8,128)S(1)}, f32[512,512]{0,1:T(8,128)}, u32[]{:S(2)}) copy-start(f32[512,512]{0,1:T(8,128)} %all-gather.34.cloned.1.call-done) | copy-start | bytes 3145732
  708.9 34.1 %collective-permute-start.7 = (f32[512,640]{1,0:T(8,128)}, f32[512,640]{1,0:T(8,128)S(1)}, u32[]{:S(2)}, u32[]{:S(2)}) collective-permute-start(f32[512,640]{1,0:T(8,128)} %fusion.68), channel_id=1, source_target_pairs={{0,16},{2,18},{4,20},{6,22},{8,24},{10,26},{12,28},{14,30},{1,17},... | collective-permute-start | bytes 3932168 | tf_op jit(solution)/shard_map/ppermute | solution.py:15
  710.1 62.1 %collective-permute-start.8 = (f32[512,640]{1,0:T(8,128)}, f32[512,640]{1,0:T(8,128)}, u32[]{:S(2)}, u32[]{:S(2)}) collective-permute-start(f32[512,640]{1,0:T(8,128)} %fusion.68), channel_id=1, source_target_pairs={{16,0},{18,2},{20,4},{22,6},{24,8},{26,10},{28,12},{30,14},{17,1},... | collective-permute-start | bytes 3932168 | tf_op jit(solution)/shard_map/ppermute | solution.py:15
  716.8 73.0 %all-gather.38.cloned.1.call-start = ((), (), s32[]{:S(2)}) async-start(), calls=%async_computation.12 | async-start | bytes 1572864 | tf_op jit(solution)/shard_map/all_gather | solution.py:123
  746.4 29.8 %copy-start.3 = (f32[512,256]{0,1:T(8,128)S(1)}, f32[512,256]{0,1:T(8,128)}, u32[]{:S(2)}) copy-start(f32[512,256]{0,1:T(8,128)} %subtract_subtract_fusion) | copy-start | bytes 1572868
  879.4 26.6 %copy-start.19 = (f32[128,128]{1,0:T(8,128)S(1)}, f32[128,128]{1,0:T(8,128)}, u32[]{:S(2)}) copy-start(f32[128,128]{1,0:T(8,128)} %fusion.281) | copy-start | bytes 196612
  (14 other events, 180.9 us)
Sparse Core Ops, SparseCore 0:
  27.4 8.5 all-gather.15
  37.6 10.3 all-gather.13
  163.0 9.4 all-gather.17
  231.2 9.2 all-gather.21
  241.9 10.2 all-gather.19
  355.2 10.3 all-gather.23
  424.2 10.1 all-gather.27
  435.9 10.3 all-gather.25
  547.8 11.2 all-gather.29
  590.5 10.1 all-gather.33
  602.3 10.3 all-gather.31
  716.9 10.1 all-gather.35
  777.3 12.4 all-gather.37
where the time goes:
time: 931 us; the launch traced here: 918 us
  other arithmetic  500 us (54%)
  waiting for transfers between devices  246 us (26%)
  matrix products  99.4 us (11%)
  starting transfers between devices  33.4 us (4%)
  local copies, waits for them, and re-layouts  23.6 us (3%)
  between operations  15.6 us (2%)
    another operation x60, other arithmetic, factor_inverse(): factor = jnp.linalg.cholesky(matrix)  263 us
    another operation x40, other arithmetic, factor_inverse(): return lax.linalg.triangular_solve(factor, unit, left_side=True, lower=True)  213 us
    ppermute x9, waiting for transfers between devices, from_behind(): return lax.ppermute(shard, axis, pairs)  198 us
    all_gather x4, waiting for transfers between devices, on_device(): lax.all_gather(diag_panel, 'col', axis=1, tiled=True)  33.7 us
    ppermute x9, starting transfers between devices, from_behind(): return lax.ppermute(shard, axis, pairs)  31.5 us
  transfers between devices with their start and end apart: 22, of which 11 were waited for; matrix products, arithmetic and copies ran while one was open for 51% of the time, Pallas kernels for 0%

commit v1 on v0

--- a/solution.py
+++ b/solution.py
@@ -1,12 +1,119 @@
+import functools
+
 import jax
 import jax.numpy as jnp
 from jax import lax
+from jax.experimental import pallas as pl
+from jax.experimental.pallas import tpu as pltpu
 from jax.sharding import PartitionSpec as P
 
 LEVELS = 6
 
 
-leaf_limit = 128
+LEAF = 128
+GROUP = 8
+
+
+def split(x):
+    high = x.astype(jnp.bfloat16)
+    low = (x - high.astype(jnp.float32)).astype(jnp.bfloat16)
+    return high, low
+
+
+def dot_split(a, b):
+    (ah, al), (bh, bl) = a, b
+    mul = functools.partial(jnp.dot, preferred_element_type=jnp.float32)
+    return mul(ah, bh) + (mul(ah, bl) + mul(al, bh))
+
+
+def dot3(a, b):
+    return dot_split(split(a), split(b))
+
+
+def leaf_inverse(blocks):
+    shape = (GROUP, LEAF)
+    lane = lax.broadcasted_iota(jnp.int32, shape, 1)
+    sub = lax.broadcasted_iota(jnp.int32, shape, 0)
+    count = LEAF // GROUP
+    sets = [[b[GROUP * i : GROUP * (i + 1), :] for i in range(count)] for b in blocks]
+
+    def row_of(v, p):
+        return jnp.broadcast_to(v[p : p + 1, :], shape)
+
+    def col_of(v, c):
+        return jnp.broadcast_to(v[:, c : c + 1], shape)
+
+    for k in range(count):
+        base = GROUP * k
+        for rows in sets:
+            v = rows[k]
+            cols = [col_of(v, base + p) for p in range(GROUP)]
+            for p in range(GROUP):
+                inv = 1.0 / row_of(cols[p], p)
+                here = sub == p
+                unit = jnp.where(here, 1.0, 0.0)
+                v = jnp.where(lane == base + p, unit, v)
+                scaled = row_of(v, p) * inv
+                v = jnp.where(here, scaled, v - cols[p] * scaled)
+                for q in range(p + 1, GROUP):
+                    entry = row_of(cols[q], p) * inv
+                    cols[q] = jnp.where(here, entry, cols[q] - cols[p] * entry)
+            rows[k] = v
+            pivots = [row_of(v, p) for p in range(GROUP)]
+            inside = (lane >= base) & (lane < base + GROUP)
+            order = list(range(k + 1, count)) + list(range(k))
+            for i in order:
+                w = rows[i]
+                acc = jnp.where(inside, 0.0, w)
+                for p in range(GROUP):
+                    acc = acc - col_of(w, base + p) * pivots[p]
+                rows[i] = acc
+    return [jnp.concatenate(rows, axis=0) for rows in sets]
+
+
+def inverse_in(work_refs):
+    n = work_refs[0].shape[-1]
+    steps = n // LEAF
+
+    def shifted_update(ref, src, dst, leaf):
+        row = ref[src, :LEAF, LEAF:]
+        col = ref[src, LEAF:, :LEAF]
+        ls = split(leaf)
+        cs = split(col)
+        q = dot_split(ls, split(row))
+        qs = split(q)
+        ref[dst, : n - LEAF, : n - LEAF] = ref[src, LEAF:, LEAF:] - dot_split(cs, qs)
+        ref[dst, n - LEAF :, : n - LEAF] = q
+        ref[dst, : n - LEAF, n - LEAF :] = -dot_split(cs, ls)
+        ref[dst, n - LEAF :, n - LEAF :] = leaf
+
+    def body(step, leaves):
+        src = lax.rem(step, 2)
+        dst = 1 - src
+        for ref, leaf in zip(work_refs, leaves):
+            shifted_update(ref, src, dst, leaf)
+        return tuple(leaf_inverse([ref[dst, :LEAF, :LEAF] for ref in work_refs]))
+
+    leaves = tuple(leaf_inverse([ref[0, :LEAF, :LEAF] for ref in work_refs]))
+    leaves = lax.fori_loop(0, steps - 1, body, leaves)
+    for ref, leaf in zip(work_refs, leaves):
+        shifted_update(ref, (steps - 1) % 2, steps % 2, leaf)
+
+
+def inverse_kernel(a_ref, o_ref, work):
+    work[0] = a_ref[...]
+    inverse_in([work])
+    o_ref[...] = work[0]
+
+
+def inverse(a):
+    n = a.shape[0]
+    return pl.pallas_call(
+        inverse_kernel,
+        out_shape=jax.ShapeDtypeStruct((n, n), jnp.float32),
+        scratch_shapes=[pltpu.VMEM((2, n, n), jnp.float32)],
+        compiler_params=pltpu.CompilerParams(vmem_limit_bytes=48 * 1024 * 1024),
+    )(a)
 
 
 def from_behind(shard, axis, by):
@@ -15,55 +122,9 @@
     return lax.ppermute(shard, axis, pairs)
 
 
-def factor_inverse(matrix):
-    width = matrix.shape[-1]
-    if width <= leaf_limit:
-        factor = jnp.linalg.cholesky(matrix)
-        unit = jnp.eye(width, dtype=matrix.dtype)
-        return lax.linalg.triangular_solve(factor, unit, left_side=True, lower=True)
-    half_w = width // 2
-    top_left = matrix[:half_w, :half_w]
-    bottom_left = matrix[half_w:, :half_w]
-    bottom_right = matrix[half_w:, half_w:]
-    first_inv = factor_inverse(top_left)
-    lower_part = jnp.dot(
-        bottom_left,
-        first_inv.T,
-        precision=lax.Precision.HIGHEST,
-        preferred_element_type=jnp.float32,
-    )
-    schur_part = bottom_right - jnp.dot(
-        lower_part,
-        lower_part.T,
-        precision=lax.Precision.HIGHEST,
-        preferred_element_type=jnp.float32,
-    )
-    second_inv = factor_inverse(schur_part)
-    cross = -jnp.dot(
-        second_inv,
-        jnp.dot(
-            lower_part,
-            first_inv,
-            precision=lax.Precision.HIGHEST,
-            preferred_element_type=jnp.float32,
-        ),
-        precision=lax.Precision.HIGHEST,
-        preferred_element_type=jnp.float32,
-    )
-    upper_row = jnp.concatenate(
-        [first_inv, jnp.zeros((half_w, width - half_w), jnp.float32)], axis=1
-    )
-    lower_row = jnp.concatenate([cross, second_inv], axis=1)
-    return jnp.concatenate([upper_row, lower_row], axis=0)
-
-
 def solve_spd(matrix, rhs):
-    inverse = factor_inverse(matrix)
-    inner = jnp.dot(
-        inverse, rhs, precision=lax.Precision.HIGHEST, preferred_element_type=jnp.float32
-    )
     return jnp.dot(
-        inverse.T, inner, precision=lax.Precision.HIGHEST, preferred_element_type=jnp.float32
+        inverse(matrix), rhs, precision=lax.Precision.HIGHEST, preferred_element_type=jnp.float32
     )
 
 

time: 931 us -> 463 us (0.50)
  the two profiles are of different devices: /device:TPU:16 before, /device:TPU:0 now
where the time goes in v1:
time: 463 us; the launch traced here: 454 us
  waiting for transfers between devices  239 us (52%)
  Pallas kernels  92.9 us (20%)
  matrix products  50.2 us (11%)
  starting transfers between devices  42.2 us (9%)
  between operations  13.9 us (3%)
  other arithmetic  9.17 us (2%)
  local copies, waits for them, and re-layouts  6.48 us (1%)
    ppermute x9, waiting for transfers between devices, from_behind(): return lax.ppermute(shard, axis, pairs)  187 us
    pallas_call x5, Pallas kernels, inverse(): pl.pallas_call(inverse_kernel, out_shape=jax.ShapeDtypeStruct((n, n), jnp...  92.9 us
    all_gather x4, waiting for transfers between devices, on_device(): lax.all_gather(diag_panel, 'col', axis=1, tiled=True)  38.9 us
    ppermute x9, starting transfers between devices, from_behind(): return lax.ppermute(shard, axis, pairs)  29.6 us
    dot_general x4, matrix products, on_device(): jnp.dot(full_upper, from_above, precision=lax.Precision.HIGHEST, preferre...  16.9 us
    dot_general x5, matrix products, solve_spd(): jnp.dot(inverse(matrix), rhs, precision=lax.Precision.HIGHEST, preferred_...  16.8 us
    dot_general x4, matrix products, on_device(): jnp.dot(full_lower, from_below, precision=lax.Precision.HIGHEST, preferre...  16.5 us
    all_gather x4, starting transfers between devices, on_device(): lax.all_gather(diag_panel, 'col', axis=1, tiled=True)  12.1 us
  transfers between devices with their start and end apart: 22, of which 12 were waited for; matrix products, arithmetic and copies ran while one was open for 7% of the time, Pallas kernels for 16%

profile of v1, /device:TPU:0, one launch (start us, length us, event | category | flops | bytes accessed | tf_op | source)
XLA Modules:
  0.0 453.7 jit_solution(2875386812668542343)
XLA Ops:
  8.7 4.9 %collective-permute-start = (f32[512,256]{1,0:T(8,128)S(1)}, f32[512,256]{1,0:T(8,128)S(1)}, u32[]{:S(2)}, u32[]{:S(2)}) collective-permute-start(f32[512,256]{1,0:T(8,128)S(1)} %get-tuple-element.6), channel_id=1, source_target_pairs={{0,2},{2,4},{4,6},{6,8},{8,10},{10,12},{12,14},{14,16},{16,18},{18... | collective-permute-start | bytes 1572872 | tf_op jit(solution)/shard_map/ppermute | solution.py:122
  13.6 11.1 %collective-permute-done = f32[512,256]{1,0:T(8,128)S(1)} collective-permute-done((f32[512,256]{1,0:T(8,128)S(1)}, f32[512,256]{1,0:T(8,128)S(1)}, u32[]{:S(2)}, u32[]{:S(2)}) %collective-permute-start) | collective-permute-done | bytes 524320 | tf_op jit(solution)/shard_map/ppermute | solution.py:122
  26.6 10.6 %all-gather.16.cloned.1.call-done.a_ref = f32[512,512]{1,0:T(8,128)} async-done(((f32[512,256]{1,0:T(8,128)}), f32[512,512]{1,0:T(8,128)}) %all-gather.16.cloned.1.call-update) | async-done | bytes 1048592 | tf_op jit(solution)/shard_map/all_gather | solution.py:159
  38.5 18.5 %shard_map.46 = f32[512,512]{1,0:T(8,128)S(1)} custom-call(f32[512,512]{1,0:T(8,128)S(1)} %copy-done.3), custom_call_target="tpu_custom_call" | custom-call | tf_op jit(solution)/shard_map/pallas_call | solution.py:111
  66.2 55.1 %collective-permute-done.1 = f32[512,640]{1,0:T(8,128)S(1)} collective-permute-done((f32[512,640]{1,0:T(8,128)}, f32[512,640]{1,0:T(8,128)S(1)}, u32[]{:S(2)}, u32[]{:S(2)}) %collective-permute-start.1) | collective-permute-done | bytes 1310752 | tf_op jit(solution)/shard_map/ppermute | solution.py:122
  121.4 3.9 fusion.31
  125.3 4.4 fusion.32
  131.7 8.5 %all-gather.22.cloned.1.call-done.a_ref = f32[512,512]{1,0:T(8,128)} async-done(((f32[512,256]{1,0:T(8,128)}), f32[512,512]{1,0:T(8,128)}) %all-gather.22.cloned.1.call-update) | async-done | bytes 1048592 | tf_op jit(solution)/shard_map/all_gather | solution.py:159
  141.4 18.5 %shard_map.47 = f32[512,512]{1,0:T(8,128)S(1)} custom-call(f32[512,512]{1,0:T(8,128)S(1)} %copy-done.2), custom_call_target="tpu_custom_call" | custom-call | tf_op jit(solution)/shard_map/pallas_call | solution.py:111
  160.0 3.8 fusion.6
  165.1 5.6 %collective-permute-start.3 = (f32[512,640]{1,0:T(8,128)}, f32[512,640]{1,0:T(8,128)}, u32[]{:S(2)}, u32[]{:S(2)}) collective-permute-start(f32[512,640]{1,0:T(8,128)} %fusion.6), channel_id=1, source_target_pairs={{0,4},{2,6},{4,8},{6,10},{8,12},{10,14},{12,16},{14,18},{16,20},{1... | collective-permute-start | bytes 3932168 | tf_op jit(solution)/shard_map/ppermute | solution.py:122
  170.7 11.3 %all-gather.28.cloned.1.call-start = ((), (), s32[]{:S(2)}) async-start(), calls=%async_computation.7 | async-start | bytes 1572864 | tf_op jit(solution)/shard_map/all_gather | solution.py:159
  182.1 14.9 %collective-permute-done.4 = f32[512,640]{1,0:T(8,128)} collective-permute-done((f32[512,640]{1,0:T(8,128)}, f32[512,640]{1,0:T(8,128)}, u32[]{:S(2)}, u32[]{:S(2)}) %collective-permute-start.4) | collective-permute-done | bytes 1310752 | tf_op jit(solution)/shard_map/ppermute | solution.py:122
  197.0 4.3 fusion.34
  201.3 23.9 %collective-permute-done.3 = f32[512,640]{1,0:T(8,128)} collective-permute-done((f32[512,640]{1,0:T(8,128)}, f32[512,640]{1,0:T(8,128)}, u32[]{:S(2)}, u32[]{:S(2)}) %collective-permute-start.3) | collective-permute-done | bytes 1310752 | tf_op jit(solution)/shard_map/ppermute | solution.py:122
  225.2 4.3 fusion.33
  232.5 11.9 %all-gather.28.cloned.1.call-done.a_ref = f32[512,512]{1,0:T(8,128)} async-done(((f32[512,256]{1,0:T(8,128)}), f32[512,512]{1,0:T(8,128)}) %all-gather.28.cloned.1.call-update) | async-done | bytes 1048592 | tf_op jit(solution)/shard_map/all_gather | solution.py:159
  245.7 18.5 %shard_map.48 = f32[512,512]{1,0:T(8,128)S(1)} custom-call(f32[512,512]{1,0:T(8,128)S(1)} %copy-done), custom_call_target="tpu_custom_call" | custom-call | tf_op jit(solution)/shard_map/pallas_call | solution.py:111
  264.2 3.8 fusion.12
  269.3 5.6 %collective-permute-start.5 = (f32[512,640]{1,0:T(8,128)}, f32[512,640]{1,0:T(8,128)}, u32[]{:S(2)}, u32[]{:S(2)}) collective-permute-start(f32[512,640]{1,0:T(8,128)} %fusion.12), channel_id=1, source_target_pairs={{0,8},{2,10},{4,12},{6,14},{8,16},{10,18},{12,20},{14,22},{16,24},... | collective-permute-start | bytes 3932168 | tf_op jit(solution)/shard_map/ppermute | solution.py:122
  275.4 25.7 %collective-permute-done.6 = f32[512,640]{1,0:T(8,128)S(1)} collective-permute-done((f32[512,640]{1,0:T(8,128)}, f32[512,640]{1,0:T(8,128)S(1)}, u32[]{:S(2)}, u32[]{:S(2)}) %collective-permute-start.6) | collective-permute-done | bytes 1310752 | tf_op jit(solution)/shard_map/ppermute | solution.py:122
  301.1 3.9 fusion.36
  305.0 4.4 fusion.35
  312.1 7.9 %all-gather.34.cloned.1.call-done.a_ref = f32[512,512]{1,0:T(8,128)} async-done(((f32[512,256]{1,0:T(8,128)}), f32[512,512]{1,0:T(8,128)}) %all-gather.34.cloned.1.call-update) | async-done | bytes 1048592 | tf_op jit(solution)/shard_map/all_gather | solution.py:159
  321.2 18.5 %shard_map.49 = f32[512,512]{1,0:T(8,128)S(1)} custom-call(f32[512,512]{1,0:T(8,128)S(1)} %copy-done.1), custom_call_target="tpu_custom_call" | custom-call | tf_op jit(solution)/shard_map/pallas_call | solution.py:111
  343.6 4.6 %collective-permute-start.7 = (f32[512,640]{1,0:T(8,128)}, f32[512,640]{1,0:T(8,128)S(1)}, u32[]{:S(2)}, u32[]{:S(2)}) collective-permute-start(f32[512,640]{1,0:T(8,128)} %fusion.18), channel_id=1, source_target_pairs={{0,16},{2,18},{4,20},{6,22},{8,24},{10,26},{12,28},{14,30},{1,17},... | collective-permute-start | bytes 3932168 | tf_op jit(solution)/shard_map/ppermute | solution.py:122
  349.8 27.2 %collective-permute-done.7 = f32[512,640]{1,0:T(8,128)S(1)} collective-permute-done((f32[512,640]{1,0:T(8,128)}, f32[512,640]{1,0:T(8,128)S(1)}, u32[]{:S(2)}, u32[]{:S(2)}) %collective-permute-start.7) | collective-permute-done | bytes 1310752 | tf_op jit(solution)/shard_map/ppermute | solution.py:122
  377.0 3.9 fusion.37
  381.0 29.2 %collective-permute-done.8 = f32[512,640]{1,0:T(8,128)} collective-permute-done((f32[512,640]{1,0:T(8,128)}, f32[512,640]{1,0:T(8,128)}, u32[]{:S(2)}, u32[]{:S(2)}) %collective-permute-start.8) | collective-permute-done | bytes 1310752 | tf_op jit(solution)/shard_map/ppermute | solution.py:122
  410.1 4.3 fusion.38
  415.4 9.9 %all-gather.38.cloned.1.call-done.a_ref = f32[512,512]{1,0:T(8,128)} async-done(((f32[512,256]{1,0:T(8,128)}), f32[512,512]{1,0:T(8,128)}) %all-gather.38.cloned.1.call-update) | async-done | bytes 1048592 | tf_op jit(solution)/shard_map/all_gather | solution.py:184
  426.5 18.7 %shard_map.50 = f32[512,512]{1,0:T(8,128)S(1)} custom-call(f32[512,512]{1,0:T(8,128)S(1)} %copy-done.4), custom_call_target="tpu_custom_call" | custom-call | tf_op jit(solution)/shard_map/pallas_call | solution.py:111
  (98 shorter events, 37.9 us)
Async XLA Ops:
  6.5 30.7 %all-gather.16.cloned.1.call-start = ((), (), s32[]{:S(2)}) async-start(), calls=%async_computation.1 | async-start | bytes 1572864 | tf_op jit(solution)/shard_map/all_gather | solution.py:159
  8.7 48.3 %copy-start.6 = (f32[512,256]{1,0:T(8,128)}, f32[512,256]{1,0:T(8,128)S(1)}, u32[]{:S(2)}) copy-start(f32[512,256]{1,0:T(8,128)S(1)} %get-tuple-element.5) | copy-start | bytes 1572868
  8.7 16.0 %collective-permute-start = (f32[512,256]{1,0:T(8,128)S(1)}, f32[512,256]{1,0:T(8,128)S(1)}, u32[]{:S(2)}, u32[]{:S(2)}) collective-permute-start(f32[512,256]{1,0:T(8,128)S(1)} %get-tuple-element.6), channel_id=1, source_target_pairs={{0,2},{2,4},{4,6},{6,8},{8,10},{10,12},{12,14},{14,16},{16,18},{18... | collective-permute-start | bytes 1572872 | tf_op jit(solution)/shard_map/ppermute | solution.py:122
  25.8 40.4 %all-gather.14.cloned.1.call-start = ((), (), s32[]{:S(2)}) async-start(), calls=%async_computation | async-start | bytes 1572864 | tf_op jit(solution)/shard_map/all_gather | solution.py:160
  25.9 31.2 %copy-start.5 = (f32[512,256]{1,0:T(8,128)S(1)}, f32[512,256]{1,0:T(8,128)}, u32[]{:S(2)}) copy-start(f32[512,256]{1,0:T(8,128)} %get-tuple-element.16) | copy-start | bytes 1572868
  26.6 98.7 %all-gather.18.cloned.1.call-start = ((), (), s32[]{:S(2)}) async-start(), calls=%async_computation.2 | async-start | bytes 1572864 | tf_op jit(solution)/shard_map/all_gather | solution.py:161
  38.5 18.6 %copy-start.19 = (f32[1,512,128]{2,1,0:T(8,128)S(1)}, f32[1,512,128]{2,1,0:T(8,128)}, u32[]{:S(2)}) copy-start(f32[1,512,128]{2,1,0:T(8,128)} %param.7) | copy-start | bytes 786436
  60.9 60.5 %collective-permute-start.1 = (f32[512,640]{1,0:T(8,128)}, f32[512,640]{1,0:T(8,128)S(1)}, u32[]{:S(2)}, u32[]{:S(2)}) collective-permute-start(f32[512,640]{1,0:T(8,128)} %fusion), channel_id=1, source_target_pairs={{0,2},{2,4},{4,6},{6,8},{8,10},{10,12},{12,14},{14,16},{16,18},{18... | collective-permute-start | bytes 3932168 | tf_op jit(solution)/shard_map/ppermute | solution.py:122
  64.6 60.8 %collective-permute-start.2 = (f32[512,640]{1,0:T(8,128)}, f32[512,640]{1,0:T(8,128)}, u32[]{:S(2)}, u32[]{:S(2)}) collective-permute-start(f32[512,640]{1,0:T(8,128)} %fusion), channel_id=1, source_target_pairs={{2,0},{4,2},{6,4},{8,6},{10,8},{12,10},{14,12},{16,14},{18,16},{20... | collective-permute-start | bytes 3932168 | tf_op jit(solution)/shard_map/ppermute | solution.py:122
  65.9 74.3 %all-gather.22.cloned.1.call-start = ((), (), s32[]{:S(2)}) async-start(), calls=%async_computation.4 | async-start | bytes 1572864 | tf_op jit(solution)/shard_map/all_gather | solution.py:159
  131.0 51.1 %all-gather.24.cloned.1.call-start = ((), (), s32[]{:S(2)}) async-start(), calls=%async_computation.5 | async-start | bytes 1572864 | tf_op jit(solution)/shard_map/all_gather | solution.py:161
  131.6 69.7 %all-gather.20.cloned.1.call-start = ((), (), s32[]{:S(2)}) async-start(), calls=%async_computation.3 | async-start | bytes 1572864 | tf_op jit(solution)/shard_map/all_gather | solution.py:160
  131.7 32.1 %copy-start.17 = (f32[512,128]{1,0:T(8,128)}, f32[512,128]{1,0:T(8,128)S(1)}, u32[]{:S(2)}) copy-start(f32[512,128]{1,0:T(8,128)S(1)} %slice_subtract_fusion.16) | copy-start | bytes 786436
  163.8 33.2 %collective-permute-start.4 = (f32[512,640]{1,0:T(8,128)}, f32[512,640]{1,0:T(8,128)}, u32[]{:S(2)}, u32[]{:S(2)}) collective-permute-start(f32[512,640]{1,0:T(8,128)} %fusion.6), channel_id=1, source_target_pairs={{4,0},{6,2},{8,4},{10,6},{12,8},{14,10},{16,12},{18,14},{20,16},{2... | collective-permute-start | bytes 3932168 | tf_op jit(solution)/shard_map/ppermute | solution.py:122
  165.1 60.1 %collective-permute-start.3 = (f32[512,640]{1,0:T(8,128)}, f32[512,640]{1,0:T(8,128)}, u32[]{:S(2)}, u32[]{:S(2)}) collective-permute-start(f32[512,640]{1,0:T(8,128)} %fusion.6), channel_id=1, source_target_pairs={{0,4},{2,6},{4,8},{6,10},{8,12},{10,14},{12,16},{14,18},{16,20},{1... | collective-permute-start | bytes 3932168 | tf_op jit(solution)/shard_map/ppermute | solution.py:122
  170.7 73.7 %all-gather.28.cloned.1.call-start = ((), (), s32[]{:S(2)}) async-start(), calls=%async_computation.7 | async-start | bytes 1572864 | tf_op jit(solution)/shard_map/all_gather | solution.py:159
  201.3 28.2 %copy-start.16 = (f32[512,256]{1,0:T(8,128)S(1)}, f32[512,256]{1,0:T(8,128)}, u32[]{:S(2)}) copy-start(f32[512,256]{1,0:T(8,128)} %get-tuple-element.14) | copy-start | bytes 1572868
  230.7 33.5 %copy-start.8 = (f32[512,256]{1,0:T(8,128)}, f32[512,256]{1,0:T(8,128)S(1)}, u32[]{:S(2)}) copy-start(f32[512,256]{1,0:T(8,128)S(1)} %get-tuple-element.10) | copy-start | bytes 1572868
  230.7 44.7 %all-gather.30.cloned.1.call-start = ((), (), s32[]{:S(2)}) async-start(), calls=%async_computation.8 | async-start | bytes 1572864 | tf_op jit(solution)/shard_map/all_gather | solution.py:161
  231.5 73.6 %all-gather.26.cloned.1.call-start = ((), (), s32[]{:S(2)}) async-start(), calls=%async_computation.6 | async-start | bytes 1572864 | tf_op jit(solution)/shard_map/all_gather | solution.py:160
  268.0 33.1 %collective-permute-start.6 = (f32[512,640]{1,0:T(8,128)}, f32[512,640]{1,0:T(8,128)S(1)}, u32[]{:S(2)}, u32[]{:S(2)}) collective-permute-start(f32[512,640]{1,0:T(8,128)} %fusion.12), channel_id=1, source_target_pairs={{8,0},{10,2},{12,4},{14,6},{16,8},{18,10},{20,12},{22,14},{24,16},... | collective-permute-start | bytes 3932168 | tf_op jit(solution)/shard_map/ppermute | solution.py:122
  269.3 35.8 %collective-permute-start.5 = (f32[512,640]{1,0:T(8,128)}, f32[512,640]{1,0:T(8,128)}, u32[]{:S(2)}, u32[]{:S(2)}) collective-permute-start(f32[512,640]{1,0:T(8,128)} %fusion.12), channel_id=1, source_target_pairs={{0,8},{2,10},{4,12},{6,14},{8,16},{10,18},{12,20},{14,22},{16,24},... | collective-permute-start | bytes 3932168 | tf_op jit(solution)/shard_map/ppermute | solution.py:122
  274.9 45.1 %all-gather.34.cloned.1.call-start = ((), (), s32[]{:S(2)}) async-start(), calls=%async_computation.10 | async-start | bytes 1572864 | tf_op jit(solution)/shard_map/all_gather | solution.py:159
  310.6 29.2 %copy-start.9 = (f32[512,256]{1,0:T(8,128)}, f32[512,256]{1,0:T(8,128)S(1)}, u32[]{:S(2)}) copy-start(f32[512,256]{1,0:T(8,128)S(1)} %get-tuple-element.9) | copy-start | bytes 1572868
  310.6 39.2 %all-gather.32.cloned.1.call-start = ((), (), s32[]{:S(2)}) async-start(), calls=%async_computation.9 | async-start | bytes 1572864 | tf_op jit(solution)/shard_map/all_gather | solution.py:160
  311.3 69.6 %all-gather.36.cloned.1.call-start = ((), (), s32[]{:S(2)}) async-start(), calls=%async_computation.11 | async-start | bytes 1572864 | tf_op jit(solution)/shard_map/all_gather | solution.py:161
  321.2 18.6 %copy-start.12 = (f32[512,256]{1,0:T(8,128)S(1)}, f32[512,256]{1,0:T(8,128)}, u32[]{:S(2)}) copy-start(f32[512,256]{1,0:T(8,128)} %get-tuple-element.7) | copy-start | bytes 1572868
  321.2 18.6 %copy-start.18 = (f32[512,128]{1,0:T(8,128)S(1)}, f32[512,128]{1,0:T(8,128)}, u32[]{:S(2)}) copy-start(f32[512,128]{1,0:T(8,128)} %slice_subtract_fusion.12) | copy-start | bytes 786436
  343.6 33.4 %collective-permute-start.7 = (f32[512,640]{1,0:T(8,128)}, f32[512,640]{1,0:T(8,128)S(1)}, u32[]{:S(2)}, u32[]{:S(2)}) collective-permute-start(f32[512,640]{1,0:T(8,128)} %fusion.18), channel_id=1, source_target_pairs={{0,16},{2,18},{4,20},{6,22},{8,24},{10,26},{12,28},{14,30},{1,17},... | collective-permute-start | bytes 3932168 | tf_op jit(solution)/shard_map/ppermute | solution.py:122
  348.2 61.9 %collective-permute-start.8 = (f32[512,640]{1,0:T(8,128)}, f32[512,640]{1,0:T(8,128)}, u32[]{:S(2)}, u32[]{:S(2)}) collective-permute-start(f32[512,640]{1,0:T(8,128)} %fusion.18), channel_id=1, source_target_pairs={{16,0},{18,2},{20,4},{22,6},{24,8},{26,10},{28,12},{30,14},{17,1},... | collective-permute-start | bytes 3932168 | tf_op jit(solution)/shard_map/ppermute | solution.py:122
  349.6 75.7 %all-gather.38.cloned.1.call-start = ((), (), s32[]{:S(2)}) async-start(), calls=%async_computation.12 | async-start | bytes 1572864 | tf_op jit(solution)/shard_map/all_gather | solution.py:184
  380.9 33.6 %copy-start.14 = (f32[512,256]{1,0:T(8,128)S(1)}, f32[512,256]{1,0:T(8,128)}, u32[]{:S(2)}) copy-start(f32[512,256]{1,0:T(8,128)} %get-tuple-element.8) | copy-start | bytes 1572868
  (11 other events, 88.0 us)
Sparse Core Ops, SparseCore 0:
  26.0 11.2 all-gather.15
  38.8 10.2 all-gather.13
  66.0 12.1 all-gather.17
  131.2 9.0 all-gather.21
  141.6 10.2 all-gather.23
  170.9 9.2 all-gather.19
  230.8 13.5 all-gather.27
  246.0 10.1 all-gather.29
  275.1 8.2 all-gather.25
  310.7 9.2 all-gather.33
  321.6 10.1 all-gather.31
  349.7 12.1 all-gather.35
  415.5 9.6 all-gather.37
